TPU v7x, 32 devices: a whole 2x2x4 slice. The times are simulated.
32 devices in a mesh: groups: 2 (over y), dp: 4 (over z), tensor: 4 (over x, core).
Axes of the slice: x: 2, y: 2, z: 4, core: 2. Of those that a mesh axis runs over, the one named last changes fastest.
Arguments:
- acts: bfloat16 [16, 192, 8192], P(('groups', 'dp'), None, 'tensor'), parts along dimension 0, may hold values from -6 to 6
- grads: bfloat16 [16, 192, 28672], P(('groups', 'dp'), None, 'tensor'), parts along dimension 0, may hold values from -6 to 6
- in_basis: bfloat16 [64, 8192], P(None, 'tensor'), may hold values from -0.0625 to 0.0625
- out_basis: bfloat16 [64, 28672], P(None, 'tensor'), may hold values from -0.03125 to 0.03125
- queries: bfloat16 [256, 4096], P('dp'), may hold values from -0.09375 to 0.09375
- lengths: int32 [16], P(('groups', 'dp')), parts along dimension 0, may hold values from 1 to 192, as said below
Outputs:
- scores: float32 [16, 256], P(('groups', 'dp')), parts along dimension 0
There are 2 independent parts, one for each index of `groups`. A program takes and returns all parts, laid end to end along the dimension named above; an argument that names none is the same for every part. Nothing has to cross between parts.
Inputs may be any that keep to these rules, and one draw needn't show every extreme that they name: `lengths`: the first example of every index of dp has all 192 tokens valid.
All inputs are finite; a program needn't handle non-finite values.
Results may differ from a plain program's by a relative error of at most 0.0029.
Values may be sent and summed in bfloat16 or wider, within the bound.
A program may use at most 64 MiB of HBM per device.

v0:
```python
import jax
import jax.numpy as jnp
from jax import lax
from jax.sharding import PartitionSpec as P


def outer_terms(rows, weights, rank):
    left = rows[:, :rank]
    right = rows[:, rank:]
    weighted = weights[:, :, None] * right[:, None, :]
    return jnp.einsum(
        "tei,tj->eij",
        weighted,
        left,
        precision=lax.Precision.HIGHEST,
        preferred_element_type=jnp.float32,
    )


def local(acts, grads, in_basis, out_basis, queries, lengths):
    e_dev, length, _ = acts.shape
    rank = in_basis.shape[0]
    dims = (((2,), (1,)), ((), ()))
    left = lax.dot_general(acts, in_basis, dims, preferred_element_type=jnp.float32)
    right = lax.dot_general(grads, out_basis, dims, preferred_element_type=jnp.float32)
    partial_rows = jnp.concatenate([left, right], axis=2).reshape(e_dev * length, 2 * rank)
    positions = jnp.arange(e_dev * length)
    owner = positions // length
    offset = positions % length
    member = (owner[:, None] == jnp.arange(e_dev)[None, :]) & (offset[:, None] < lengths[None, :])
    weights = member.astype(jnp.float32) * lax.rsqrt(lengths.astype(jnp.float32))[None, :]
    summed = lax.psum(partial_rows, "tensor")
    sketch = outer_terms(summed, weights, rank)
    flat = sketch.reshape(e_dev, rank * rank).astype(jnp.bfloat16)
    contract = (((1,), (1,)), ((), ()))
    return lax.dot_general(
        flat,
        lax.all_gather(queries, "dp", axis=0, tiled=True),
        contract,
        preferred_element_type=jnp.float32,
    )


def solution(mesh):
    in_specs = (
        P(("groups", "dp"), None, "tensor"),
        P(("groups", "dp"), None, "tensor"),
        P(None, "tensor"),
        P(None, "tensor"),
        P("dp", None),
        P(("groups", "dp")),
    )
    out_specs = P(("groups", "dp"), None)
    return jax.shard_map(local, mesh=mesh, in_specs=in_specs, out_specs=out_specs, check_vma=False)
```

profile of v0, /device:TPU:0, one launch (start us, length us, event | category | flops | bytes accessed | tf_op | source)
XLA Modules:
  0.0 74.5 jit_solution(2874785727629088002)
XLA Ops:
  7.4 0.0 copy-start
  7.4 0.0 copy-start.1
  7.4 0.0 all-reduce.2.cloned.1.call-start
  7.4 4.8 %fusion = f32[2,192,64]{1,2,0:T(8,128)S(1)} fusion(bf16[2,192,7168]{2,1,0:T(8,128)(2,1)} %param.7, bf16[64,7168]{1,0:T(8,128)(2,1)} %param.9), kind=kOutput, calls=%fused_computation.1 | convolution fusion | flops 352321536 | bytes 6520832 | tf_op jit(solution)/shard_map/dot_general | solution.py:25
  12.2 0.0 copy-done
  12.2 0.0 copy-done.1
  12.2 0.0 copy-start.2
  12.2 0.6 fusion.2
  12.8 0.1 copy.7
  13.0 0.8 %copy.8 = f32[384,128]{0,1:T(8,128)} copy(f32[384,128]{1,0:T(8,128)S(1)} %bitcast.14) | data formatting | bytes 393216 | tf_op jit(solution)/shard_map/reshape | solution.py:26
  13.8 0.0 all-reduce.2.cloned.1.call-update
  13.8 0.0 all-gather.2.cloned.1.call-start
  13.9 0.5 all-gather.2.cloned.1.call-update
  14.4 0.0 copy-done.2
  14.4 0.1 and_select_fusion
  14.5 33.9 %all-reduce.2.cloned.1.call-done = f32[384,128]{0,1:T(8,128)} async-done(((f32[384,128]{0,1:T(8,128)}), f32[384,128]{0,1:T(8,128)}) %all-reduce.2.cloned.1.call-update) | async-done | bytes 196624 | tf_op jit(solution)/shard_map/psum | solution.py:32
  48.5 0.9 %slice.8 = f32[384,64]{0,1:T(8,128)S(1)} slice(f32[384,128]{0,1:T(8,128)} %all-reduce.2.cloned.1.call-done), slice={[0:384], [64:128]} | slice | bytes 196608 | tf_op jit(solution)/shard_map/slice | solution.py:9
  49.4 1.2 %convolution_convert_fusion = bf16[2,64,64]{2,1,0:T(8,128)(2,1)S(1)} fusion(f32[384,128]{0,1:T(8,128)} %all-reduce.2.cloned.1.call-done, f32[384,64]{0,1:T(8,128)S(1)} %slice.8, f32[384,2]{0,1:T(2,128)S(1)} %and_select_fusion), kind=kOutput, calls=%fused_computation | convolution fusion | flops 37806080 | bytes 216064 | tf_op jit(solution)/shard_map/tei,tj->eij/dot_general | solution.py:11
  50.6 0.1 convert_element_type.12
  50.7 13.6 %all-gather.2.cloned.1.call-done = bf16[256,4096]{1,0:T(8,128)(2,1)} async-done(((bf16[64,4096]{1,0:T(8,128)(2,1)}), bf16[256,4096]{1,0:T(8,128)(2,1)}) %all-gather.2.cloned.1.call-update) | async-done | bytes 2097168 | tf_op jit(solution)/shard_map/all_gather | solution.py:38
  64.2 2.8 %fusion.14 = f32[2,256]{1,0:T(2,128)} fusion(bf16[2,4096]{1,0:T(2,128)(2,1)S(1)} %convert_element_type.12, bf16[256,4096]{1,0:T(8,128)(2,1)} %all-gather.2.cloned.1.call-done), kind=kOutput, calls=%fused_computation.23 | convolution fusion | flops 4194304 | bytes 2115584 | tf_op jit(solution)/shard_map/dot_general | solution.py:36
  (3 shorter events, 0.0 us)
Async XLA Ops:
  7.4 4.8 %copy-start = (bf16[2,192,2048]{2,1,0:T(8,128)(2,1)S(1)}, bf16[2,192,2048]{2,1,0:T(8,128)(2,1)}, u32[]{:S(2)}) copy-start(bf16[2,192,2048]{2,1,0:T(8,128)(2,1)} %param.6) | copy-start | bytes 4718596
  7.4 4.8 %copy-start.1 = (bf16[64,2048]{1,0:T(8,128)(2,1)S(1)}, bf16[64,2048]{1,0:T(8,128)(2,1)}, u32[]{:S(2)}) copy-start(bf16[64,2048]{1,0:T(8,128)(2,1)} %param.8) | copy-start | bytes 786436
  7.4 41.1 %all-reduce.2.cloned.1.call-start = ((), (), s32[]{:S(2)}) async-start(), calls=%async_computation | async-start | bytes 393216 | tf_op jit(solution)/shard_map/psum | solution.py:32
  12.2 2.2 %copy-start.2 = (s32[2]{0:T(128)S(1)}, s32[2]{0:T(128)}, u32[]{:S(2)}) copy-start(s32[2]{0:T(128)} %param.11) | copy-start | bytes 28
  13.8 50.4 %all-gather.2.cloned.1.call-start = ((), (), s32[]{:S(2)}) async-start(), calls=%async_computation.1 | async-start | bytes 2621440 | tf_op jit(solution)/shard_map/all_gather | solution.py:38
Sparse Core Ops, SparseCore 0:
  13.9 34.4 all-reduce.1
Sparse Core Ops, SparseCore 1:
  15.9 48.2 all-gather.1
where the time goes:
time: 74.7 us; the launch traced here: 74.5 us
  waiting for transfers between devices  48 us (64%)
  between operations  14.9 us (20%)
  matrix products  9.43 us (13%)
  local copies, waits for them, and re-layouts  1.95 us (3%)
    psum x1, waiting for transfers between devices, local(): summed = lax.psum(partial_rows, 'tensor')  33.9 us
    all_gather x1, waiting for transfers between devices, local(): lax.all_gather(queries, 'dp', axis=0, tiled=True)  13.6 us
    dot_general x1, matrix products, local(): lax.dot_general(grads, out_basis, dims, preferred_element_type=jnp.float32)  4.79 us
    dot_general x1, matrix products, local(): lax.dot_general(flat, lax.all_gather(queries, 'dp', axis=0, tiled=True),...  2.82 us
  transfers between devices with their start and end apart: 2, of which 2 were waited for; matrix products, arithmetic and copies ran while one was open for 3% of the time, Pallas kernels for 0%

commit v1 on v0

v1 whole, which is shorter than its diff:
```python
import functools

import jax
import jax.numpy as jnp
from jax import lax
from jax.experimental import pallas as pl
from jax.experimental.pallas import tpu as pltpu
from jax.sharding import PartitionSpec as P

MESH = pl.DeviceIdType.MESH
NT = (((1,), (1,)), ((), ()))
LANES = 128


def each(start, stop, body):
    if stop - start <= 16:
        for s in range(start, stop):
            body(s)
    else:
        lax.fori_loop(start, stop, lambda s, c: (body(s), c)[1], 0)


def kernel(
    nd, n,
    acts, grads, in_basis, out_basis, queries, lengths,
    out,
    acts_v, grads_v, ib_v, ob_v, q_v,
    row_send, row_recv, sketch_v, part_v, part_recv, sum_v, score_send, score_recv,
    acts_sem, grads_sem, basis_sem, row_ssem, row_rsem, part_ssem, part_rsem, score_ssem, score_rsem,
):
    z = lax.axis_index("dp")
    k = lax.axis_index("tensor")
    e_dev, length, _ = acts.shape
    rank = in_basis.shape[0]
    parts = n // e_dev
    rows = length // parts
    mine, c = k // parts, lax.rem(k, parts)
    feats = q_v.shape[1]
    nq = queries.shape[0]
    peers = nd * n
    me = z * n + k

    def owner(s):
        return lax.rem(k + s, n)

    def fetch(src, dst, sem, s):
        b = owner(s)
        return pltpu.make_async_copy(
            src.at[b // parts, pl.ds(pl.multiple_of(lax.rem(b, parts) * rows, rows), rows), :],
            dst.at[s], sem.at[s])

    order = [s % n for s in range(1, n + 1)]
    get_ib = pltpu.make_async_copy(in_basis, ib_v, basis_sem.at[0])
    get_ob = pltpu.make_async_copy(out_basis, ob_v, basis_sem.at[1])
    get_q = pltpu.make_async_copy(
        queries.at[:, pl.ds(pl.multiple_of(c * feats, feats), feats)], q_v, basis_sem.at[2])
    get_ib.start()
    for s in order:
        fetch(acts, acts_v, acts_sem, s).start()
    get_ob.start()
    for s in order:
        fetch(grads, grads_v, grads_sem, s).start()
    get_q.start()

    barrier = pltpu.get_barrier_semaphore()

    def greet(s):
        to = lax.rem(me + s, peers)
        pl.semaphore_signal(
            barrier, inc=1, device_id={"dp": to // n, "tensor": lax.rem(to, n)}, device_id_type=MESH)

    each(1, peers, greet)

    def row_copy(s, side):
        return pltpu.make_async_remote_copy(
            src_ref=row_send.at[side, s], dst_ref=row_recv.at[side, s],
            send_sem=row_ssem.at[side, s], recv_sem=row_rsem.at[side, s],
            device_id={"tensor": owner(s)}, device_id_type=MESH)

    get_ib.wait()
    for s in order:
        fetch(acts, acts_v, acts_sem, s).wait()
        row_send[0, s] = lax.dot_general(ib_v[...], acts_v[s], NT, preferred_element_type=jnp.float32)
    pl.semaphore_wait(barrier, peers - 1)
    for s in range(1, n):
        row_copy(s, 0).start()

    get_ob.wait()
    for s in order:
        fetch(grads, grads_v, grads_sem, s).wait()
        row_send[1, s] = lax.dot_general(ob_v[...], grads_v[s], NT, preferred_element_type=jnp.float32)
        if s:
            row_copy(s, 1).start()

    left, right = row_send[0, 0], row_send[1, 0]
    for s in range(1, n):
        row_copy(s, 0).wait()
        left = left + row_recv[0, s]
    count = jnp.full((1, rows), lengths[mine], jnp.int32)
    place = c * rows + lax.broadcasted_iota(jnp.int32, (1, rows), 1)
    weight = jnp.where(place < count, lax.rsqrt(count.astype(jnp.float32)), 0.0)
    left = left * weight
    left = jnp.concatenate([left, left], axis=0)
    for s in range(1, n):
        row_copy(s, 1).wait()
        right = right + row_recv[1, s]
    sketch_v[...] = lax.dot_general(
        right, left, NT, precision=lax.Precision.HIGHEST, preferred_element_type=jnp.float32)

    lines = rank * rank // LANES
    per = LANES // rank
    lane = lax.broadcasted_iota(jnp.int32, (lines, LANES), 1)
    flat = sketch_v[pl.ds(0, lines, stride=per), :]
    for p in range(1, per):
        flat = jnp.where(lane < p * rank, flat, sketch_v[pl.ds(p, lines, stride=per), :])
    piece = lines // parts
    for p in range(parts):
        part_v[p] = flat[p * piece:(p + 1) * piece]

    group = nd * parts
    g = z * parts + c

    def part_copy(s, slot):
        to = lax.rem(g + s, group)
        return pltpu.make_async_remote_copy(
            src_ref=part_v.at[lax.rem(to, parts)], dst_ref=part_recv.at[slot],
            send_sem=part_ssem.at[s], recv_sem=part_rsem.at[s],
            device_id={"dp": to // parts, "tensor": mine * parts + lax.rem(to, parts)}, device_id_type=MESH)

    each(1, group, lambda s: part_copy(s, g).start())
    part_recv[g] = part_v[c]
    each(1, group, lambda s: part_copy(s, lax.rem(g - s + group, group)).wait())

    def add_parts(d):
        total = part_recv[d * parts]
        for p in range(1, parts):
            total = total + part_recv[d * parts + p]
        sum_v[pl.ds(d * piece, piece), :] = total

    for d in range(nd):
        add_parts(d)
    sketch = jnp.concatenate(
        [sum_v[pl.ds(r, nd, stride=piece), :] for r in range(piece)], axis=1).astype(jnp.bfloat16)
    get_q.wait()
    scores = lax.dot_general(sketch, q_v[...], NT, preferred_element_type=jnp.float32)

    width = score_send.shape[-1]
    fit = width // nq
    if fit > 1:
        scores = jnp.concatenate([scores] * fit, axis=1)
        lane = lax.broadcasted_iota(jnp.int32, scores.shape, 1)
        first = lax.rem(z, fit) * nq
        scores = jnp.where((lane >= first) & (lane < first + nq), scores, 0.0)
    for d in range(nd):
        score_send[d] = scores[d:d + 1]

    def score_copy(s, slot):
        to = lax.rem(me + s, peers)
        return pltpu.make_async_remote_copy(
            src_ref=score_send.at[to // n], dst_ref=score_recv.at[slot],
            send_sem=score_ssem.at[s], recv_sem=score_rsem.at[s],
            device_id={"dp": to // n, "tensor": lax.rem(to, n)}, device_id_type=MESH)

    each(1, peers, lambda s: score_copy(s, me).start())
    score_recv[me] = score_send[z]
    each(1, peers, lambda s: score_copy(s, lax.rem(me - s + peers, peers)).wait())
    for line in range(nd // fit):
        for e in range(e_dev):
            total = None
            for d in range(line * fit, (line + 1) * fit):
                for p in range(parts):
                    term = score_recv[d * n + e * parts + p]
                    total = term if total is None else total + term
            out[e:e + 1, line * width:(line + 1) * width] = total


def local(nd, n, acts, grads, in_basis, out_basis, queries, lengths):
    e_dev, length, ka = acts.shape
    kg = grads.shape[2]
    rank = in_basis.shape[0]
    parts = n // e_dev
    rows = length // parts
    nq, feats = queries.shape
    lines = rank * rank // LANES
    width = max(LANES, nq)
    f32, bf16 = jnp.float32, jnp.bfloat16
    hbm = pl.BlockSpec(memory_space=pl.ANY)
    dma = pltpu.SemaphoreType.DMA
    return pl.pallas_call(
        functools.partial(kernel, nd, n),
        out_shape=jax.ShapeDtypeStruct((e_dev, nd * nq), f32),
        in_specs=[hbm] * 5 + [pl.BlockSpec(memory_space=pltpu.SMEM)],
        out_specs=pl.BlockSpec(memory_space=pltpu.VMEM),
        scratch_shapes=[
            pltpu.VMEM((n, rows, ka), bf16),
            pltpu.VMEM((n, rows, kg), bf16),
            pltpu.VMEM((rank, ka), bf16),
            pltpu.VMEM((rank, kg), bf16),
            pltpu.VMEM((nq, feats // parts), bf16),
            pltpu.VMEM((2, n, rank, rows), f32),
            pltpu.VMEM((2, n, rank, rows), f32),
            pltpu.VMEM((rank, LANES), f32),
            pltpu.VMEM((parts, lines // parts, LANES), f32),
            pltpu.VMEM((nd * parts, lines // parts, LANES), f32),
            pltpu.VMEM((nd * lines // parts, LANES), f32),
            pltpu.VMEM((nd, 1, width), f32),
            pltpu.VMEM((nd * n, 1, width), f32),
            dma((n,)),
            dma((n,)),
            dma((3,)),
            dma((2, n)),
            dma((2, n)),
            dma((nd * parts,)),
            dma((nd * parts,)),
            dma((nd * n,)),
            dma((nd * n,)),
        ],
        compiler_params=pltpu.CompilerParams(
            collective_id=0, has_side_effects=True, vmem_limit_bytes=48 * 2**20),
        cost_estimate=pl.CostEstimate(
            flops=2 * e_dev * length * rank * (ka + kg),
            bytes_accessed=2 * (e_dev * length + rank) * (ka + kg) + 2 * nq * feats // parts,
            transcendentals=0),
    )(acts, grads, in_basis, out_basis, queries, lengths)


def solution(mesh):
    nd, n = mesh.shape["dp"], mesh.shape["tensor"]
    in_specs = (
        P(("groups", "dp"), None, "tensor"),
        P(("groups", "dp"), None, "tensor"),
        P(None, "tensor"),
        P(None, "tensor"),
        P("dp", None),
        P(("groups", "dp")),
    )
    out_specs = P(("groups", "dp"), None)
    return jax.shard_map(
        functools.partial(local, nd, n), mesh=mesh, in_specs=in_specs, out_specs=out_specs, check_vma=False)
```

time: 74.7 us -> 27.9 us (0.37)
  waiting for transfers between devices: 48 us -> 0 us
  Pallas kernels: 0 us -> 21.8 us
  between operations: 14.9 us -> 0.01 us
  matrix products: 9.43 us -> 0 us
  local copies, waits for them, and re-layouts: 1.95 us -> 5.81 us
    psum x1 -> x0, waiting for transfers between devices: 33.9 us -> none  [local(): summed = lax.psum(partial_rows, 'tensor')]
    pallas_call x0 -> x1, Pallas kernels: none -> 21.8 us  [local(): pl.pallas_call(functools.partial(kernel, nd, n), out_shape=jax.ShapeDtype...]
    all_gather x1 -> x0, waiting for transfers between devices: 13.6 us -> none  [local(): lax.all_gather(queries, 'dp', axis=0, tiled=True)]
    dot_general x4 -> x0, matrix products: 9.43 us -> none  [the longest x1 4.79 us: local(): lax.dot_general(grads, out_basis, dims, preferred_element_type=jnp.float32)]
    unnamed x6 -> x11, local copies, waits for them, and re-layouts: 0.01 us -> 5.81 us
    slice x1 -> x0, local copies, waits for them, and re-layouts: 0.9 us -> none  [outer_terms(): right = rows[:, rank:]]
    reshape x1 -> x0, local copies, waits for them, and re-layouts: 0.82 us -> none  [local(): jnp.concatenate([left, right], axis=2).reshape(e_dev * length, 2 * rank)]
  transfers between devices with their start and end apart: 2 -> 0, of which waited for: 2 -> 0; matrix products, arithmetic and copies ran while one was open for 3% -> 0% of each run, Pallas kernels for 0% -> 0%
where the time goes in v1:
time: 27.9 us; the launch traced here: 27.6 us
  Pallas kernels  21.8 us (78%)
  local copies, waits for them, and re-layouts  5.81 us (21%)
    pallas_call x1, Pallas kernels, local(): pl.pallas_call(functools.partial(kernel, nd, n), out_shape=jax.ShapeDtype...  21.8 us
    unnamed x11, local copies, waits for them, and re-layouts  5.81 us

profile of v1, /device:TPU:0, one launch (start us, length us, event | category | flops | bytes accessed | tf_op | source)
XLA Modules:
  0.0 27.6 jit_solution(1273950595046738229)
XLA Ops:
  0.0 0.0 copy-start
  0.0 1.4 %copy-done = bf16[2,192,2048]{2,1,0:T(8,128)(2,1)S(1)} copy-done((bf16[2,192,2048]{2,1,0:T(8,128)(2,1)S(1)}, bf16[2,192,2048]{2,1,0:T(8,128)(2,1)}, u32[]{:S(2)}) %copy-start) | copy-done | bytes 1572888
  1.4 0.0 copy-start.1
  1.4 1.2 %copy-done.1 = bf16[64,7168]{1,0:T(8,128)(2,1)S(1)} copy-done((bf16[64,7168]{1,0:T(8,128)(2,1)S(1)}, bf16[64,7168]{1,0:T(8,128)(2,1)}, u32[]{:S(2)}) %copy-start.1) | copy-done | bytes 917528
  2.6 0.0 copy-start.2
  2.6 1.0 %copy-done.2 = bf16[64,4096]{1,0:T(8,128)(2,1)S(1)} copy-done((bf16[64,4096]{1,0:T(8,128)(2,1)S(1)}, bf16[64,4096]{1,0:T(8,128)(2,1)}, u32[]{:S(2)}) %copy-start.2) | copy-done | bytes 524312
  3.6 0.0 copy-start.3
  3.6 0.9 %copy-done.3 = bf16[64,2048]{1,0:T(8,128)(2,1)S(1)} copy-done((bf16[64,2048]{1,0:T(8,128)(2,1)S(1)}, bf16[64,2048]{1,0:T(8,128)(2,1)}, u32[]{:S(2)}) %copy-start.3) | copy-done | bytes 262168
  4.6 0.0 copy-start.4
  4.6 0.7 %copy-done.4 = s32[2]{0:T(128)S(1)} copy-done((s32[2]{0:T(128)S(1)}, s32[2]{0:T(128)}, u32[]{:S(2)}) %copy-start.4) | copy-done | bytes 32
  5.2 21.8 %shard_map.64 = f32[2,256]{1,0:T(2,128)S(1)} custom-call(bf16[2,192,2048]{2,1,0:T(8,128)(2,1)S(1)} %copy-done, bf16[2,192,7168]{2,1,0:T(8,128)(2,1)} %grads.1, bf16[64,2048]{1,0:T(8,128)(2,1)S(1)} %copy-done.3, bf16[64,7168]{1,0:T(8,128)(2,1)S(1)} %copy-done.1, bf16[64,4096]{1,0:T(8,128)(2,1)S(1)} %copy-done.2, s32[2]{0:T(128)S(1)} %copy-done.4), custom_call_target="tpu_custom_call" | custom-call | flops 452984832 | bytes 8519680 | tf_op jit(solution)/shard_map/pallas_call | solution.py:189
  27.0 0.6 %copy.8 = f32[2,256]{1,0:T(2,128)} copy(f32[2,256]{1,0:T(2,128)S(1)} %shard_map.64) | data formatting | bytes 4096
Async XLA Ops:
  0.0 1.4 %copy-start = (bf16[2,192,2048]{2,1,0:T(8,128)(2,1)S(1)}, bf16[2,192,2048]{2,1,0:T(8,128)(2,1)}, u32[]{:S(2)}) copy-start(bf16[2,192,2048]{2,1,0:T(8,128)(2,1)} %acts.1) | copy-start | bytes 4718596
  1.4 1.2 %copy-start.1 = (bf16[64,7168]{1,0:T(8,128)(2,1)S(1)}, bf16[64,7168]{1,0:T(8,128)(2,1)}, u32[]{:S(2)}) copy-start(bf16[64,7168]{1,0:T(8,128)(2,1)} %out_basis.1) | copy-start | bytes 2752516
  2.6 1.0 %copy-start.2 = (bf16[64,4096]{1,0:T(8,128)(2,1)S(1)}, bf16[64,4096]{1,0:T(8,128)(2,1)}, u32[]{:S(2)}) copy-start(bf16[64,4096]{1,0:T(8,128)(2,1)} %queries.1) | copy-start | bytes 1572868
  3.6 0.9 %copy-start.3 = (bf16[64,2048]{1,0:T(8,128)(2,1)S(1)}, bf16[64,2048]{1,0:T(8,128)(2,1)}, u32[]{:S(2)}) copy-start(bf16[64,2048]{1,0:T(8,128)(2,1)} %in_basis.1) | copy-start | bytes 786436
  4.6 0.7 %copy-start.4 = (s32[2]{0:T(128)S(1)}, s32[2]{0:T(128)}, u32[]{:S(2)}) copy-start(s32[2]{0:T(128)} %lengths.1) | copy-start | bytes 28

commit v2 on v1

--- a/solution.py
+++ b/solution.py
@@ -10,6 +10,8 @@
 MESH = pl.DeviceIdType.MESH
 NT = (((1,), (1,)), ((), ()))
 LANES = 128
+DEPTH = 2
+HELD = 1
 
 
 def each(start, stop, body):
@@ -24,7 +26,7 @@
     nd, n,
     acts, grads, in_basis, out_basis, queries, lengths,
     out,
-    acts_v, grads_v, ib_v, ob_v, q_v,
+    acts_v, grads_v, ib_v, ob_v, q_v, len_v,
     row_send, row_recv, sketch_v, part_v, part_recv, sum_v, score_send, score_recv,
     acts_sem, grads_sem, basis_sem, row_ssem, row_rsem, part_ssem, part_rsem, score_ssem, score_rsem,
 ):
@@ -54,13 +56,13 @@
     get_ob = pltpu.make_async_copy(out_basis, ob_v, basis_sem.at[1])
     get_q = pltpu.make_async_copy(
         queries.at[:, pl.ds(pl.multiple_of(c * feats, feats), feats)], q_v, basis_sem.at[2])
+    get_len = pltpu.make_async_copy(lengths, len_v, basis_sem.at[3])
     get_ib.start()
     for s in order:
         fetch(acts, acts_v, acts_sem, s).start()
     get_ob.start()
-    for s in order:
+    for s in order[:DEPTH]:
         fetch(grads, grads_v, grads_sem, s).start()
-    get_q.start()
 
     barrier = pltpu.get_barrier_semaphore()
 
@@ -81,28 +83,37 @@
     for s in order:
         fetch(acts, acts_v, acts_sem, s).wait()
         row_send[0, s] = lax.dot_general(ib_v[...], acts_v[s], NT, preferred_element_type=jnp.float32)
-    pl.semaphore_wait(barrier, peers - 1)
-    for s in range(1, n):
-        row_copy(s, 0).start()
-
     get_ob.wait()
-    for s in order:
+    for i, s in enumerate(order):
         fetch(grads, grads_v, grads_sem, s).wait()
+        if i + DEPTH < n:
+            fetch(grads, grads_v, grads_sem, order[i + DEPTH]).start()
+        elif i == n - 1:
+            get_q.start()
+            get_len.start()
         row_send[1, s] = lax.dot_general(ob_v[...], grads_v[s], NT, preferred_element_type=jnp.float32)
-        if s:
+        if i == HELD:
+            pl.semaphore_wait(barrier, peers - 1)
+            for t in range(1, n):
+                row_copy(t, 0).start()
+            for t in order[:i + 1]:
+                if t:
+                    row_copy(t, 1).start()
+        elif i > HELD and s:
             row_copy(s, 1).start()
 
     left, right = row_send[0, 0], row_send[1, 0]
     for s in range(1, n):
-        row_copy(s, 0).wait()
+        row_copy(s, 0).wait_recv()
         left = left + row_recv[0, s]
-    count = jnp.full((1, rows), lengths[mine], jnp.int32)
+    get_len.wait()
+    count = jnp.full((1, rows), len_v[mine], jnp.int32)
     place = c * rows + lax.broadcasted_iota(jnp.int32, (1, rows), 1)
     weight = jnp.where(place < count, lax.rsqrt(count.astype(jnp.float32)), 0.0)
     left = left * weight
     left = jnp.concatenate([left, left], axis=0)
     for s in range(1, n):
-        row_copy(s, 1).wait()
+        row_copy(s, 1).wait_recv()
         right = right + row_recv[1, s]
     sketch_v[...] = lax.dot_general(
         right, left, NT, precision=lax.Precision.HIGHEST, preferred_element_type=jnp.float32)
@@ -129,7 +140,7 @@
 
     each(1, group, lambda s: part_copy(s, g).start())
     part_recv[g] = part_v[c]
-    each(1, group, lambda s: part_copy(s, lax.rem(g - s + group, group)).wait())
+    each(1, group, lambda s: part_copy(s, lax.rem(g - s + group, group)).wait_recv())
 
     def add_parts(d):
         total = part_recv[d * parts]
@@ -163,7 +174,7 @@
 
     each(1, peers, lambda s: score_copy(s, me).start())
     score_recv[me] = score_send[z]
-    each(1, peers, lambda s: score_copy(s, lax.rem(me - s + peers, peers)).wait())
+    each(1, peers, lambda s: score_copy(s, lax.rem(me - s + peers, peers)).wait_recv())
     for line in range(nd // fit):
         for e in range(e_dev):
             total = None
@@ -172,6 +183,12 @@
                     term = score_recv[d * n + e * parts + p]
                     total = term if total is None else total + term
             out[e:e + 1, line * width:(line + 1) * width] = total
+
+    for s in range(1, n):
+        row_copy(s, 0).wait_send()
+        row_copy(s, 1).wait_send()
+    each(1, group, lambda s: part_copy(s, g).wait_send())
+    each(1, peers, lambda s: score_copy(s, me).wait_send())
 
 
 def local(nd, n, acts, grads, in_basis, out_basis, queries, lengths):
@@ -184,12 +201,12 @@
     lines = rank * rank // LANES
     width = max(LANES, nq)
     f32, bf16 = jnp.float32, jnp.bfloat16
-    hbm = pl.BlockSpec(memory_space=pl.ANY)
+    hbm = pl.BlockSpec(memory_space=pltpu.HBM)
     dma = pltpu.SemaphoreType.DMA
     return pl.pallas_call(
         functools.partial(kernel, nd, n),
         out_shape=jax.ShapeDtypeStruct((e_dev, nd * nq), f32),
-        in_specs=[hbm] * 5 + [pl.BlockSpec(memory_space=pltpu.SMEM)],
+        in_specs=[hbm] * 6,
         out_specs=pl.BlockSpec(memory_space=pltpu.VMEM),
         scratch_shapes=[
             pltpu.VMEM((n, rows, ka), bf16),
@@ -197,6 +214,7 @@
             pltpu.VMEM((rank, ka), bf16),
             pltpu.VMEM((rank, kg), bf16),
             pltpu.VMEM((nq, feats // parts), bf16),
+            pltpu.SMEM((e_dev,), jnp.int32),
             pltpu.VMEM((2, n, rank, rows), f32),
             pltpu.VMEM((2, n, rank, rows), f32),
             pltpu.VMEM((rank, LANES), f32),
@@ -207,7 +225,7 @@
             pltpu.VMEM((nd * n, 1, width), f32),
             dma((n,)),
             dma((n,)),
-            dma((3,)),
+            dma((4,)),
             dma((2, n)),
             dma((2, n)),
             dma((nd * parts,)),
@@ -216,7 +234,7 @@
             dma((nd * n,)),
         ],
         compiler_params=pltpu.CompilerParams(
-            collective_id=0, has_side_effects=True, vmem_limit_bytes=48 * 2**20),
+            collective_id=0, has_side_effects=True, vmem_limit_bytes=60 * 2**20),
         cost_estimate=pl.CostEstimate(
             flops=2 * e_dev * length * rank * (ka + kg),
             bytes_accessed=2 * (e_dev * length + rank) * (ka + kg) + 2 * nq * feats // parts,

time: 27.9 us -> 21.6 us (0.77)
  local copies, waits for them, and re-layouts: 5.81 us -> 1.26 us
  Pallas kernels: 21.8 us -> 20.2 us
    unnamed x11 -> x1, local copies, waits for them, and re-layouts: 5.81 us -> 1.26 us
    pallas_call x1, Pallas kernels: 21.8 us -> 20.2 us  [local(): pl.pallas_call(functools.partial(kernel, nd, n), out_shape=jax.ShapeDtype...]
where the time goes in v2:
time: 21.6 us; the launch traced here: 21.5 us
  Pallas kernels  20.2 us (94%)
  local copies, waits for them, and re-layouts  1.26 us (6%)
    pallas_call x1, Pallas kernels, local(): pl.pallas_call(functools.partial(kernel, nd, n), out_shape=jax.ShapeDtype...  20.2 us
    unnamed x1, local copies, waits for them, and re-layouts  1.26 us

profile of v2, /device:TPU:0, one launch (start us, length us, event | category | flops | bytes accessed | tf_op | source)
XLA Modules:
  0.0 21.5 jit_solution(5542173990418061924)
XLA Ops:
  0.0 20.2 %shard_map.64 = f32[2,256]{1,0:T(2,128)} custom-call(bf16[2,192,2048]{2,1,0:T(8,128)(2,1)} %acts.1, bf16[2,192,7168]{2,1,0:T(8,128)(2,1)} %grads.1, bf16[64,2048]{1,0:T(8,128)(2,1)} %in_basis.1, bf16[64,7168]{1,0:T(8,128)(2,1)} %out_basis.1, bf16[64,4096]{1,0:T(8,128)(2,1)} %queries.1, s32[2]{0:T(128)} %lengths.1), custom_call_target="tpu_custom_call" | custom-call | flops 452984832 | bytes 8519680 | tf_op jit(solution)/shard_map/pallas_call | solution.py:206
  20.2 1.3 %copy.8 = f32[2,256]{1,0:T(2,128)} copy(f32[2,256]{1,0:T(2,128)} %shard_map.64) | data formatting | bytes 4096

commit v3 on v2

--- a/solution.py
+++ b/solution.py
@@ -42,8 +42,11 @@
     peers = nd * n
     me = z * n + k
 
+    half = lax.rem(k, 2)
+
     def owner(s):
-        return lax.rem(k + s, n)
+        pair, flip = s // 2, s % 2
+        return lax.rem(k // 2 + pair, n // 2) * 2 + (lax.rem(half + 1, 2) if flip else half)
 
     def fetch(src, dst, sem, s):
         b = owner(s)
@@ -51,7 +54,7 @@
             src.at[b // parts, pl.ds(pl.multiple_of(lax.rem(b, parts) * rows, rows), rows), :],
             dst.at[s], sem.at[s])
 
-    order = [s % n for s in range(1, n + 1)]
+    order = [s for s in range(2, n)] + [1, 0]
     get_ib = pltpu.make_async_copy(in_basis, ib_v, basis_sem.at[0])
     get_ob = pltpu.make_async_copy(out_basis, ob_v, basis_sem.at[1])
     get_q = pltpu.make_async_copy(
@@ -73,16 +76,16 @@
 
     each(1, peers, greet)
 
-    def row_copy(s, side):
+    def row_copy(s):
         return pltpu.make_async_remote_copy(
-            src_ref=row_send.at[side, s], dst_ref=row_recv.at[side, s],
-            send_sem=row_ssem.at[side, s], recv_sem=row_rsem.at[side, s],
+            src_ref=row_send.at[s], dst_ref=row_recv.at[s],
+            send_sem=row_ssem.at[s], recv_sem=row_rsem.at[s],
             device_id={"tensor": owner(s)}, device_id_type=MESH)
 
     get_ib.wait()
     for s in order:
         fetch(acts, acts_v, acts_sem, s).wait()
-        row_send[0, s] = lax.dot_general(ib_v[...], acts_v[s], NT, preferred_element_type=jnp.float32)
+        row_send[s, :, :rank] = lax.dot_general(acts_v[s], ib_v[...], NT, preferred_element_type=jnp.float32)
     get_ob.wait()
     for i, s in enumerate(order):
         fetch(grads, grads_v, grads_sem, s).wait()
@@ -91,32 +94,27 @@
         elif i == n - 1:
             get_q.start()
             get_len.start()
-        row_send[1, s] = lax.dot_general(ob_v[...], grads_v[s], NT, preferred_element_type=jnp.float32)
+        row_send[s, :, rank:] = lax.dot_general(grads_v[s], ob_v[...], NT, preferred_element_type=jnp.float32)
         if i == HELD:
             pl.semaphore_wait(barrier, peers - 1)
-            for t in range(1, n):
-                row_copy(t, 0).start()
             for t in order[:i + 1]:
                 if t:
-                    row_copy(t, 1).start()
+                    row_copy(t).start()
         elif i > HELD and s:
-            row_copy(s, 1).start()
-
-    left, right = row_send[0, 0], row_send[1, 0]
-    for s in range(1, n):
-        row_copy(s, 0).wait_recv()
-        left = left + row_recv[0, s]
+            row_copy(s).start()
+
+    both = row_send[0]
+    for s in order[:-1]:
+        row_copy(s).wait_recv()
+        both = both + row_recv[s]
     get_len.wait()
-    count = jnp.full((1, rows), len_v[mine], jnp.int32)
-    place = c * rows + lax.broadcasted_iota(jnp.int32, (1, rows), 1)
+    count = jnp.full((rows, 2 * rank), len_v[mine], jnp.int32)
+    place = c * rows + lax.broadcasted_iota(jnp.int32, (rows, 2 * rank), 0)
     weight = jnp.where(place < count, lax.rsqrt(count.astype(jnp.float32)), 0.0)
-    left = left * weight
-    left = jnp.concatenate([left, left], axis=0)
-    for s in range(1, n):
-        row_copy(s, 1).wait_recv()
-        right = right + row_recv[1, s]
+    left, right = both[:, :rank] * weight[:, :rank], both[:, rank:]
+    left = jnp.concatenate([left, left], axis=1)
     sketch_v[...] = lax.dot_general(
-        right, left, NT, precision=lax.Precision.HIGHEST, preferred_element_type=jnp.float32)
+        right, left, (((0,), (0,)), ((), ())), precision=lax.Precision.HIGHEST, preferred_element_type=jnp.float32)
 
     lines = rank * rank // LANES
     per = LANES // rank
@@ -185,8 +183,7 @@
             out[e:e + 1, line * width:(line + 1) * width] = total
 
     for s in range(1, n):
-        row_copy(s, 0).wait_send()
-        row_copy(s, 1).wait_send()
+        row_copy(s).wait_send()
     each(1, group, lambda s: part_copy(s, g).wait_send())
     each(1, peers, lambda s: score_copy(s, me).wait_send())
 
@@ -215,8 +212,8 @@
             pltpu.VMEM((rank, kg), bf16),
             pltpu.VMEM((nq, feats // parts), bf16),
             pltpu.SMEM((e_dev,), jnp.int32),
-            pltpu.VMEM((2, n, rank, rows), f32),
-            pltpu.VMEM((2, n, rank, rows), f32),
+            pltpu.VMEM((n, rows, 2 * rank), f32),
+            pltpu.VMEM((n, rows, 2 * rank), f32),
             pltpu.VMEM((rank, LANES), f32),
             pltpu.VMEM((parts, lines // parts, LANES), f32),
             pltpu.VMEM((nd * parts, lines // parts, LANES), f32),
@@ -226,8 +223,8 @@
             dma((n,)),
             dma((n,)),
             dma((4,)),
-            dma((2, n)),
-            dma((2, n)),
+            dma((n,)),
+            dma((n,)),
             dma((nd * parts,)),
             dma((nd * parts,)),
             dma((nd * n,)),

time: 21.6 us -> 20.9 us (0.968)
  Pallas kernels: 20.2 us -> 19.5 us
    pallas_call x1, Pallas kernels: 20.2 us -> 19.5 us  [local(): pl.pallas_call(functools.partial(kernel, nd, n), out_shape=jax.ShapeDtype...]
where the time goes in v3:
time: 20.9 us; the launch traced here: 20.8 us
  Pallas kernels  19.5 us (93%)
  local copies, waits for them, and re-layouts  1.26 us (6%)
    pallas_call x1, Pallas kernels, local(): pl.pallas_call(functools.partial(kernel, nd, n), out_shape=jax.ShapeDtype...  19.5 us
    unnamed x1, local copies, waits for them, and re-layouts  1.26 us

profile of v3, /device:TPU:0, one launch (start us, length us, event | category | flops | bytes accessed | tf_op | source)
XLA Modules:
  0.0 20.8 jit_solution(806933144254613231)
XLA Ops:
  0.0 19.5 %shard_map.64 = f32[2,256]{1,0:T(2,128)} custom-call(bf16[2,192,2048]{2,1,0:T(8,128)(2,1)} %acts.1, bf16[2,192,7168]{2,1,0:T(8,128)(2,1)} %grads.1, bf16[64,2048]{1,0:T(8,128)(2,1)} %in_basis.1, bf16[64,7168]{1,0:T(8,128)(2,1)} %out_basis.1, bf16[64,4096]{1,0:T(8,128)(2,1)} %queries.1, s32[2]{0:T(128)} %lengths.1), custom_call_target="tpu_custom_call" | custom-call | flops 452984832 | bytes 8519680 | tf_op jit(solution)/shard_map/pallas_call | solution.py:203
  19.5 1.3 %copy.8 = f32[2,256]{1,0:T(2,128)} copy(f32[2,256]{1,0:T(2,128)} %shard_map.64) | data formatting | bytes 4096

commit v4 on v3

--- a/solution.py
+++ b/solution.py
@@ -11,15 +11,32 @@
 NT = (((1,), (1,)), ((), ()))
 LANES = 128
 DEPTH = 2
-HELD = 1
+HELD = 0
 
 
 def each(start, stop, body):
     if stop - start <= 16:
-        for s in range(start, stop):
+        for s in reversed(range(start, stop)):
             body(s)
     else:
         lax.fori_loop(start, stop, lambda s, c: (body(s), c)[1], 0)
+
+
+def to_at(a, s, count):
+    if not isinstance(s, int) or count & (count - 1):
+        return lax.rem(a + s, count)
+    bit, to = 1, a
+    while bit < count:
+        if s & bit:
+            to = to + bit - 2 * bit * lax.rem(a // bit, 2)
+        bit *= 2
+    return to
+
+
+def from_at(a, s, count):
+    if not isinstance(s, int) or count & (count - 1):
+        return lax.rem(a - s + count, count)
+    return to_at(a, s, count)
 
 
 def kernel(
@@ -70,7 +87,7 @@
     barrier = pltpu.get_barrier_semaphore()
 
     def greet(s):
-        to = lax.rem(me + s, peers)
+        to = to_at(me, s, peers)
         pl.semaphore_signal(
             barrier, inc=1, device_id={"dp": to // n, "tensor": lax.rem(to, n)}, device_id_type=MESH)
 
@@ -130,7 +147,7 @@
     g = z * parts + c
 
     def part_copy(s, slot):
-        to = lax.rem(g + s, group)
+        to = to_at(g, s, group)
         return pltpu.make_async_remote_copy(
             src_ref=part_v.at[lax.rem(to, parts)], dst_ref=part_recv.at[slot],
             send_sem=part_ssem.at[s], recv_sem=part_rsem.at[s],
@@ -138,7 +155,7 @@
 
     each(1, group, lambda s: part_copy(s, g).start())
     part_recv[g] = part_v[c]
-    each(1, group, lambda s: part_copy(s, lax.rem(g - s + group, group)).wait_recv())
+    each(1, group, lambda s: part_copy(s, from_at(g, s, group)).wait_recv())
 
     def add_parts(d):
         total = part_recv[d * parts]
@@ -164,7 +181,7 @@
         score_send[d] = scores[d:d + 1]
 
     def score_copy(s, slot):
-        to = lax.rem(me + s, peers)
+        to = to_at(me, s, peers)
         return pltpu.make_async_remote_copy(
             src_ref=score_send.at[to // n], dst_ref=score_recv.at[slot],
             send_sem=score_ssem.at[s], recv_sem=score_rsem.at[s],
@@ -172,7 +189,7 @@
 
     each(1, peers, lambda s: score_copy(s, me).start())
     score_recv[me] = score_send[z]
-    each(1, peers, lambda s: score_copy(s, lax.rem(me - s + peers, peers)).wait_recv())
+    each(1, peers, lambda s: score_copy(s, from_at(me, s, peers)).wait_recv())
     for line in range(nd // fit):
         for e in range(e_dev):
             total = None

time: 20.9 us -> 20.7 us (level)
  no operation moved by 1% of the time
where the time goes in v4:
time: 20.7 us; the launch traced here: 20.5 us
  Pallas kernels  19.3 us (93%)
  local copies, waits for them, and re-layouts  1.26 us (6%)
    pallas_call x1, Pallas kernels, local(): pl.pallas_call(functools.partial(kernel, nd, n), out_shape=jax.ShapeDtype...  19.3 us
    unnamed x1, local copies, waits for them, and re-layouts  1.26 us

profile of v4, /device:TPU:0, one launch (start us, length us, event | category | flops | bytes accessed | tf_op | source)
XLA Modules:
  0.0 20.5 jit_solution(5626100112227746791)
XLA Ops:
  0.0 19.3 %shard_map.64 = f32[2,256]{1,0:T(2,128)} custom-call(bf16[2,192,2048]{2,1,0:T(8,128)(2,1)} %acts.1, bf16[2,192,7168]{2,1,0:T(8,128)(2,1)} %grads.1, bf16[64,2048]{1,0:T(8,128)(2,1)} %in_basis.1, bf16[64,7168]{1,0:T(8,128)(2,1)} %out_basis.1, bf16[64,4096]{1,0:T(8,128)(2,1)} %queries.1, s32[2]{0:T(128)} %lengths.1), custom_call_target="tpu_custom_call" | custom-call | flops 452984832 | bytes 8519680 | tf_op jit(solution)/shard_map/pallas_call | solution.py:220
  19.3 1.3 %copy.8 = f32[2,256]{1,0:T(2,128)} copy(f32[2,256]{1,0:T(2,128)} %shard_map.64) | data formatting | bytes 4096

commit v5 on v4

--- a/solution.py
+++ b/solution.py
@@ -120,14 +120,14 @@
         elif i > HELD and s:
             row_copy(s).start()
 
+    get_len.wait()
+    count = jnp.full((rows, 2 * rank), len_v[mine], jnp.int32)
+    place = c * rows + lax.broadcasted_iota(jnp.int32, (rows, 2 * rank), 0)
+    weight = jnp.where(place < count, lax.rsqrt(count.astype(jnp.float32)), 0.0)
     both = row_send[0]
     for s in order[:-1]:
         row_copy(s).wait_recv()
         both = both + row_recv[s]
-    get_len.wait()
-    count = jnp.full((rows, 2 * rank), len_v[mine], jnp.int32)
-    place = c * rows + lax.broadcasted_iota(jnp.int32, (rows, 2 * rank), 0)
-    weight = jnp.where(place < count, lax.rsqrt(count.astype(jnp.float32)), 0.0)
     left, right = both[:, :rank] * weight[:, :rank], both[:, rank:]
     left = jnp.concatenate([left, left], axis=1)
     sketch_v[...] = lax.dot_general(

time: 20.7 us -> 20.7 us (level)
  no operation moved by 1% of the time
where the time goes in v5:
time: 20.7 us; the launch traced here: 20.5 us
  Pallas kernels  19.3 us (93%)
  local copies, waits for them, and re-layouts  1.26 us (6%)
    pallas_call x1, Pallas kernels, local(): pl.pallas_call(functools.partial(kernel, nd, n), out_shape=jax.ShapeDtype...  19.3 us
    unnamed x1, local copies, waits for them, and re-layouts  1.26 us

profile of v5, /device:TPU:0, one launch (start us, length us, event | category | flops | bytes accessed | tf_op | source)
XLA Modules:
  0.0 20.5 jit_solution(1902228246068212855)
XLA Ops:
  0.0 19.3 %shard_map.64 = f32[2,256]{1,0:T(2,128)} custom-call(bf16[2,192,2048]{2,1,0:T(8,128)(2,1)} %acts.1, bf16[2,192,7168]{2,1,0:T(8,128)(2,1)} %grads.1, bf16[64,2048]{1,0:T(8,128)(2,1)} %in_basis.1, bf16[64,7168]{1,0:T(8,128)(2,1)} %out_basis.1, bf16[64,4096]{1,0:T(8,128)(2,1)} %queries.1, s32[2]{0:T(128)} %lengths.1), custom_call_target="tpu_custom_call" | custom-call | flops 452984832 | bytes 8519680 | tf_op jit(solution)/shard_map/pallas_call | solution.py:220
  19.3 1.3 %copy.8 = f32[2,256]{1,0:T(2,128)} copy(f32[2,256]{1,0:T(2,128)} %shard_map.64) | data formatting | bytes 4096
